TPU v7x, 32 devices: a whole 2x2x4 slice. The times are simulated.
32 devices in a mesh: prow: 4 (over x, core), pcol: 8 (over z, y).
Axes of the slice: x: 2, y: 2, z: 4, core: 2. Of those that a mesh axis runs over, the one named last changes fastest.
Arguments:
- inverse_blocks: bfloat16 [7168, 7168], P('prow', 'pcol'), may hold values from -6 to 6
- lower_late: bfloat16 [56, 128, 256], P('prow', 'pcol'), may hold values from -0.09375 to 0.09375
- lower_early: bfloat16 [56, 128, 256], P('prow', 'pcol'), may hold values from -0.09375 to 0.09375
- link_block: bfloat16 [256, 256], replicated, may hold values from -0.375 to 0.375
- diag_inverse: float32 [2, 256, 256], replicated, may hold values from -6 to 6
- structures: int32 [2, 28], replicated, may hold values from 0 to 55, as said below
Outputs:
- panel_late: float32 [56, 128, 256], P('prow', 'pcol')
- diag_late: float32 [256, 256], replicated
- panel_early: float32 [56, 128, 256], P('prow', 'pcol')
- cross_block: float32 [256, 256], replicated
- diag_early: float32 [256, 256], replicated
Inputs may be any that keep to these rules, and one draw needn't show every extreme that they name: `structures`: each row lists 28 different block numbers in increasing order. Among the 14 blocks with the same value of n // 14 at most 10 are listed, and in each row some such group has exactly 10.
All inputs are finite; a program needn't handle non-finite values.
Results may differ from a plain program's by a relative error of at most 0.01.
Values may be sent and summed in bfloat16 or wider, within the bound.
A program may use at most 64 MiB of HBM per device.

v0:
```python
import jax
import jax.numpy as jnp
from jax import lax
from jax.sharding import PartitionSpec as P

WIDTH = 256
BLK = 128


def from_root(value, axis, source):
    kept = jnp.where(lax.axis_index(axis) == source, value, 0).astype(value.dtype)
    return lax.psum(kept, axis)


def split_parts(values):
    upper = values.astype(jnp.bfloat16)
    lower = (values - upper.astype(jnp.float32)).astype(jnp.bfloat16)
    return (upper, lower)


def rows_product(left, right_float):
    upper, lower = split_parts(right_float)
    dims = (((0,), (0,)), ((), ()))
    first = lax.dot_general(left, upper, dims, preferred_element_type=jnp.float32)
    return first + lax.dot_general(left, lower, dims, preferred_element_type=jnp.float32)


def shards(inverse_blocks, lower_late, lower_early, link_block, diag_inverse, structures):
    high = lax.Precision.HIGHEST
    row_blocks = inverse_blocks.shape[0] // BLK
    col_blocks = inverse_blocks.shape[1] // BLK
    row_id = lax.axis_index("prow")
    col_id = lax.axis_index("pcol")
    block_ids = row_id * row_blocks + jnp.arange(row_blocks, dtype=jnp.int32)

    def block_hits(listed):
        return jnp.any(listed[:, None] == block_ids[None, :], axis=0).astype(jnp.float32)

    def own_columns(strip):
        return lax.dynamic_slice_in_dim(strip, col_id % 2 * col_blocks, col_blocks, 0)

    def reduce_columns(columns, flag_list):
        count = len(flag_list)
        product = jnp.dot(inverse_blocks, columns, preferred_element_type=jnp.float32)
        summed = lax.psum_scatter(
            product.reshape(row_blocks, BLK, count * WIDTH).astype(jnp.bfloat16),
            "pcol",
            scatter_dimension=1,
            tiled=True,
        ).astype(jnp.float32)
        return [summed]

    def separate_reduce(masked, hit_flags):
        strip = lax.all_gather(masked, "pcol", axis=1, tiled=True)
        columns = from_root(own_columns(strip), "prow", col_id // 2)
        columns = columns.reshape(col_blocks * BLK, WIDTH)
        return reduce_columns(columns, [hit_flags])[0]

    hits_late = block_hits(structures[0])
    hits_early = block_hits(structures[1])
    masked_late = lower_late * hits_late.astype(jnp.bfloat16)[:, None, None]
    masked_early = lower_early * hits_early.astype(jnp.bfloat16)[:, None, None]
    late_rows = masked_late.reshape(-1, WIDTH)
    early_rows = masked_early.reshape(-1, WIDTH)
    link_float = link_block.astype(jnp.float32)
    reduced_late = separate_reduce(masked_late, hits_late)
    reduced_early = separate_reduce(masked_early, hits_early)
    panel_late = -(reduced_late * hits_late[:, None, None])
    late_flat = panel_late.reshape(-1, WIDTH)
    local_late = rows_product(late_rows, late_flat)
    cross_local = rows_product(early_rows, late_flat).T
    sum_late = lax.psum(local_late, ("prow", "pcol"))
    diag_late = diag_inverse[0] - sum_late
    flat_upper, flat_lower = split_parts(late_flat)
    carried = jnp.dot(flat_upper, link_block, preferred_element_type=jnp.float32) + jnp.dot(
        flat_lower, link_block, preferred_element_type=jnp.float32
    )
    panel_early = -(
        (reduced_early + carried.reshape(reduced_early.shape)) * hits_early[:, None, None]
    )
    local_early = rows_product(early_rows, panel_early.reshape(-1, WIDTH))
    sum_early, cross_sum = lax.psum((local_early, cross_local), ("prow", "pcol"))
    cross_block = -cross_sum - jnp.dot(diag_late, link_float, precision=high)
    diag_early = diag_inverse[1] - sum_early - jnp.dot(link_float.T, cross_block, precision=high)
    return (panel_late, diag_late, panel_early, cross_block, diag_early)


def solution(mesh):
    placed = (P("prow", "pcol"), P("prow", "pcol", None), P("prow", "pcol", None), P(), P(), P())
    return jax.shard_map(
        shards,
        mesh=mesh,
        in_specs=placed,
        out_specs=(P("prow", "pcol", None), P(), P("prow", "pcol", None), P(), P()),
        check_vma=False,
    )
```

profile of v0, /device:TPU:0, one launch (start us, length us, event | category | flops | bytes accessed | tf_op | source)
XLA Modules:
  0.0 405.6 jit_solution(15092679226556821970)
XLA Ops:
  7.2 0.0 copy-start
  7.2 0.0 all-reduce.7.cloned.1.call-start
  7.3 0.9 slice_bitcast_fusion.1
  8.1 0.2 compare_reduce_fusion
  8.3 1.0 broadcast_multiply_fusion
  9.3 36.2 %all_gather.7 = bf16[14,128,256]{2,1,0:T(8,128)(2,1)} all-gather(bf16[14,16,256]{2,1,0:T(8,128)(2,1)S(1)} %broadcast_multiply_fusion), channel_id=1, replica_groups=mesh['prow'=4,'pcol'=8] {'pcol'}, dimensions={1}, use_global_device_ids=true | all-gather | bytes 1032192 | tf_op jit(solution)/shard_map/all_gather | solution.py:54
  45.5 1.0 broadcast_multiply_fusion.1
  46.5 0.0 copy-start.6
  46.5 0.7 copy-done.6
  47.1 34.3 %all_gather.6 = bf16[14,128,256]{2,1,0:T(8,128)(2,1)} all-gather(bf16[14,16,256]{2,1,0:T(8,128)(2,1)S(1)} %broadcast_multiply_fusion.1), channel_id=1, replica_groups=mesh['prow'=4,'pcol'=8] {'pcol'}, dimensions={1}, use_global_device_ids=true | all-gather | bytes 1032192 | tf_op jit(solution)/shard_map/all_gather | solution.py:54
  81.5 1.8 dynamic-slice_select_fusion
  83.3 1.8 dynamic-slice_select_fusion.1
  85.1 0.0 all-reduce.7.cloned.1.call-update
  85.2 0.0 reduce-scatter.3.cloned.1.call-start
  85.2 37.1 %all-reduce.7.cloned.1.call-done = (bf16[896,256]{1,0:T(8,128)(2,1)}, bf16[896,256]{1,0:T(8,128)(2,1)}) async-done(((bf16[896,256]{1,0:T(8,128)(2,1)}, bf16[896,256]{1,0:T(8,128)(2,1)}), (bf16[896,256]{1,0:T(8,128)(2,1)}, bf16[896,256]{1,0:T(8,128)(2,1)})) %all-reduce.7.cloned.1.call-update) | async-done | bytes 917520 | tf_op jit(solution)/shard_map/psum | solution.py:12
  122.3 0.0 copy-done
  122.3 3.2 fusion
  125.5 2.2 copy.17
  127.7 0.0 reduce-scatter.3.cloned.1.call-update
  127.7 0.0 reduce-scatter.5.cloned.1.call-start
  127.7 3.1 fusion.1
  130.9 0.0 copy-start.1
  130.9 2.3 copy.18
  133.1 0.0 reduce-scatter.5.cloned.1.call-update
  133.1 0.0 all-reduce.5.cloned.1.call-start
  133.2 59.1 %reduce-scatter.3.cloned.1.call-done = bf16[14,16,256]{2,1,0:T(8,128)(2,1)} async-done(((bf16[14,128,256]{2,1,0:T(8,128)(2,1)}), bf16[14,16,256]{2,1,0:T(8,128)(2,1)}) %reduce-scatter.3.cloned.1.call-update) | async-done | bytes 114704 | tf_op jit(solution)/shard_map/reduce_scatter | solution.py:45
  192.3 1.0 multiply_negate_fusion.1
  193.3 0.0 copy-start.4
  193.3 0.9 convolution_bitcast_fusion.3
  194.2 1.8 convolution_bitcast_fusion.5
  196.1 0.0 copy-done.4
  196.1 0.0 copy-done.1
  196.1 0.2 fusion.13
  196.3 0.9 convolution_add_fusion
  197.2 62.1 %reduce-scatter.5.cloned.1.call-done = bf16[14,16,256]{2,1,0:T(8,128)(2,1)} async-done(((bf16[14,128,256]{2,1,0:T(8,128)(2,1)}), bf16[14,16,256]{2,1,0:T(8,128)(2,1)}) %reduce-scatter.5.cloned.1.call-update) | async-done | bytes 114704 | tf_op jit(solution)/shard_map/reduce_scatter | solution.py:45
  259.3 0.0 copy-start.5
  259.3 0.0 copy-start.10
  259.3 0.0 copy-start.7
  259.3 0.0 copy-start.9
  259.3 1.2 multiply_negate_fusion
  260.5 0.0 copy-start.8
  260.5 0.2 convolution_bitcast_fusion.1
  260.7 0.9 fusion.5
  261.6 0.0 copy-done.5
  261.6 0.0 copy-done.10
  261.6 0.9 fusion.4
  262.6 0.0 copy-done.8
  262.6 0.0 copy-done.7
  262.6 0.0 copy-done.9
  262.6 0.9 fusion.3
  263.5 0.0 all-reduce.5.cloned.1.call-update
  263.5 130.9 %all-reduce.5.cloned.1.call-done = (f32[256,256]{1,0:T(8,128)}, f32[256,256]{1,0:T(8,128)}, f32[256,256]{1,0:T(8,128)}) async-done(((f32[256,256]{1,0:T(8,128)}, f32[256,256]{1,0:T(8,128)}, f32[256,256]{1,0:T(8,128)}), (f32[256,256]{1,0:T(8,128)}, f32[256,256]{1,0:T(8,128)}, f32[256,256]{1,0:T(8,128)})) %all-reduce.5.cloned.1.call-update) | async-done | bytes 786448 | tf_op jit(solution)/shard_map/psum | solution.py:72
  394.5 1.1 bitcast_subtract_fusion.1
  395.6 0.0 copy-start.2
  395.6 1.3 convolution_subtract_fusion
  396.9 0.0 copy-start.3
  396.9 2.1 fusion.2
  399.0 0.0 copy-done.2
  399.1 0.0 copy-done.3
  (3 shorter events, 0.0 us)
Async XLA Ops:
  7.2 115.1 %copy-start = (bf16[1792,896]{1,0:T(8,128)(2,1)S(1)}, bf16[1792,896]{1,0:T(8,128)(2,1)}, u32[]{:S(2)}) copy-start(bf16[1792,896]{1,0:T(8,128)(2,1)} %param.6) | copy-start | bytes 9633796
  7.2 115.1 %all-reduce.7.cloned.1.call-start = ((), (), s32[]{:S(2)}) async-start(), calls=%async_computation.5 | async-start | bytes 1835008 | tf_op jit(solution)/shard_map/psum | solution.py:12
  46.5 0.7 copy-start.6
  85.2 107.1 %reduce-scatter.3.cloned.1.call-start = ((), (), s32[]{:S(2)}) async-start(), calls=%async_computation.2 | async-start | bytes 1032192 | tf_op jit(solution)/shard_map/reduce_scatter | solution.py:45
  127.7 131.6 %reduce-scatter.5.cloned.1.call-start = ((), (), s32[]{:S(2)}) async-start(), calls=%async_computation.3 | async-start | bytes 1032192 | tf_op jit(solution)/shard_map/reduce_scatter | solution.py:45
  130.9 65.2 %copy-start.1 = (bf16[256,256]{1,0:T(8,128)(2,1)S(1)}, bf16[256,256]{1,0:T(8,128)(2,1)}, u32[]{:S(2)}) copy-start(bf16[256,256]{1,0:T(8,128)(2,1)} %param.9) | copy-start | bytes 393220
  133.1 261.4 %all-reduce.5.cloned.1.call-start = ((), (), s32[]{:S(2)}) async-start(), calls=%async_computation.4 | async-start | bytes 1572864 | tf_op jit(solution)/shard_map/psum | solution.py:72
  193.3 2.8 copy-start.4
  259.3 2.4 copy-start.5
  259.3 2.4 copy-start.10
  259.3 3.3 copy-start.7
  259.3 3.3 copy-start.9
  260.5 2.1 copy-start.8
  395.6 3.5 copy-start.2
  396.9 2.2 copy-start.3
Sparse Core Ops, SparseCore 0:
  85.3 36.9 all-reduce.6
  127.8 64.4 reduce-scatter.2
  196.0 63.1 reduce-scatter.4
  265.2 129.2 all-reduce.4
where the time goes:
time: 406 us
  waiting for transfers between devices  289 us (71%)
  blocking collectives  70.5 us (17%)
  matrix products  16.6 us (4%)
  between operations  13.9 us (3%)
  other arithmetic  9.06 us (2%)
  local copies, waits for them, and re-layouts  6.03 us (1%)
    psum x1, waiting for transfers between devices, shards(): sum_late = lax.psum(local_late, ('prow', 'pcol'))  131 us
    reduce_scatter x2, waiting for transfers between devices, reduce_columns(): lax.psum_scatter(product.reshape(row_blocks, BLK, count * WIDTH).astype(j...  121 us
    all_gather x2, blocking collectives, separate_reduce(): strip = lax.all_gather(masked, 'pcol', axis=1, tiled=True)  70.5 us
    psum x1, waiting for transfers between devices, from_root(): return lax.psum(kept, axis)  37.1 us
  transfers between devices with their start and end apart: 4, of which 4 were waited for; matrix products, arithmetic and copies ran while one was open for 3% of the time, Pallas kernels for 0%

commit v1 on v0

--- a/solution.py
+++ b/solution.py
@@ -51,7 +51,16 @@
         return [summed]
 
     def separate_reduce(masked, hit_flags):
-        strip = lax.all_gather(masked, "pcol", axis=1, tiled=True)
+        ways = lax.axis_size("pcol")
+        up = [(d, (d + 1) % ways) for d in range(ways)]
+        down = [(d, (d - 1) % ways) for d in range(ways)]
+        earlier, later = ([masked], [masked])
+        for _ in range(ways // 2):
+            earlier.append(lax.ppermute(earlier[-1], "pcol", up))
+        for _ in range((ways - 1) // 2):
+            later.append(lax.ppermute(later[-1], "pcol", down))
+        line = jnp.concatenate([*earlier[::-1], *later[1:]], axis=1)
+        strip = jnp.roll(line, (lax.axis_index("pcol") - ways // 2) * masked.shape[1], axis=1)
         columns = from_root(own_columns(strip), "prow", col_id // 2)
         columns = columns.reshape(col_blocks * BLK, WIDTH)
         return reduce_columns(columns, [hit_flags])[0]

time: 406 us -> 379 us (0.933)
  blocking collectives: 70.5 us -> 0 us
  starting transfers between devices: 0.16 us -> 24.9 us
  waiting for transfers between devices: 289 us -> 298 us
  local copies, waits for them, and re-layouts: 6.03 us -> 15 us
    all_gather x2 -> x0, blocking collectives: 70.5 us -> none  [separate_reduce(): strip = lax.all_gather(masked, 'pcol', axis=1, tiled=True)]
    ppermute x0 -> x14, starting transfers between devices: none -> 24.7 us  [the longest x8 13.6 us: separate_reduce(): earlier.append(lax.ppermute(earlier[-1], 'pcol', up))]
    ppermute x0 -> x14, waiting for transfers between devices: none -> 12.8 us  [the longest x8 10.4 us: separate_reduce(): earlier.append(lax.ppermute(earlier[-1], 'pcol', up))]
    unnamed x22 -> x40, local copies, waits for them, and re-layouts: 0.71 us -> 9.62 us
  transfers between devices with their start and end apart: 4 -> 18, of which waited for: 4 -> 11; matrix products, arithmetic and copies ran while one was open for 3% -> 6% of each run, Pallas kernels for 0% -> 0%
where the time goes in v1:
time: 379 us; the launch traced here: 378 us
  waiting for transfers between devices  298 us (79%)
  starting transfers between devices  24.9 us (7%)
  matrix products  16.5 us (4%)
  local copies, waits for them, and re-layouts  15 us (4%)
  between operations  14 us (4%)
  other arithmetic  9.64 us (3%)
    psum x1, waiting for transfers between devices, shards(): sum_late = lax.psum(local_late, ('prow', 'pcol'))  130 us
    reduce_scatter x2, waiting for transfers between devices, reduce_columns(): lax.psum_scatter(product.reshape(row_blocks, BLK, count * WIDTH).astype(j...  121 us
    psum x1, waiting for transfers between devices, from_root(): return lax.psum(kept, axis)  33.9 us
    ppermute x8, starting transfers between devices, separate_reduce(): earlier.append(lax.ppermute(earlier[-1], 'pcol', up))  13.6 us
    ppermute x6, starting transfers between devices, separate_reduce(): later.append(lax.ppermute(later[-1], 'pcol', down))  11.2 us
    ppermute x8, waiting for transfers between devices, separate_reduce(): earlier.append(lax.ppermute(earlier[-1], 'pcol', up))  10.4 us
    unnamed x40, local copies, waits for them, and re-layouts  9.62 us
  transfers between devices with their start and end apart: 18, of which 11 were waited for; matrix products, arithmetic and copies ran while one was open for 6% of the time, Pallas kernels for 0%

profile of v1, /device:TPU:0, one launch (start us, length us, event | category | flops | bytes accessed | tf_op | source)
XLA Modules:
  0.0 378.4 jit_solution(7036703348480872769)
XLA Ops:
  7.2 0.0 all-reduce.7.cloned.1.call-start
  7.2 0.9 slice_bitcast_fusion.1
  8.1 0.2 compare_reduce_fusion
  8.3 1.0 broadcast_multiply_fusion
  9.3 3.0 collective-permute-start.7
  12.3 1.0 broadcast_multiply_fusion.1
  13.3 1.6 collective-permute-start
  14.9 3.9 %collective-permute-done.7 = bf16[14,16,256]{2,1,0:T(8,128)(2,1)S(1)} collective-permute-done((bf16[14,16,256]{2,1,0:T(8,128)(2,1)S(1)}, bf16[14,16,256]{2,1,0:T(8,128)(2,1)S(1)}, u32[]{:S(2)}, u32[]{:S(2)}) %collective-permute-start.7) | collective-permute-done | bytes 114720 | tf_op jit(solution)/shard_map/ppermute | solution.py:59
  18.7 4.7 %collective-permute-start.11 = (bf16[14,16,256]{2,1,0:T(8,128)(2,1)S(1)}, bf16[14,16,256]{2,1,0:T(8,128)(2,1)}, u32[]{:S(2)}, u32[]{:S(2)}) collective-permute-start(bf16[14,16,256]{2,1,0:T(8,128)(2,1)S(1)} %broadcast_multiply_fusion), channel_id=1, source_target_pairs={{0,7},{1,0},{2,1},{3,2},{4,3},{5,4},{6,5},{7,6},{8,15},{9,8},{10,9... | collective-permute-start | bytes 344072 | tf_op jit(solution)/shard_map/ppermute | solution.py:61
  23.4 0.0 collective-permute-start.4
  23.5 2.0 collective-permute-start.1
  25.5 2.5 collective-permute-done.8
  28.0 2.5 collective-permute-start.9
  30.5 2.2 collective-permute-start.12
  32.7 0.5 collective-permute-done.4
  33.2 1.8 collective-permute-start.5
  35.0 0.3 collective-permute-start.2
  35.3 2.4 collective-permute-done.9
  37.6 2.8 collective-permute-start.10
  40.4 0.1 collective-permute-done.12
  40.5 1.9 collective-permute-start.13
  42.4 1.8 collective-permute-done.5
  44.2 0.6 collective-permute-start.6
  44.8 1.5 collective-permute-start.3
  46.2 0.9 constant_dynamic-update-slice_fusion.15
  47.1 0.9 constant_dynamic-update-slice_fusion.14
  48.0 0.9 constant_dynamic-update-slice_fusion.13
  48.9 0.9 constant_dynamic-update-slice_fusion.12
  49.9 1.0 constant_dynamic-update-slice_fusion.11
  50.8 1.6 collective-permute-done.3
  52.5 0.9 constant_dynamic-update-slice_fusion.6
  53.4 0.9 constant_dynamic-update-slice_fusion.5
  54.3 0.9 constant_dynamic-update-slice_fusion.4
  55.2 1.0 constant_dynamic-update-slice_fusion.3
  56.2 0.9 constant_dynamic-update-slice_fusion.10
  57.1 0.9 constant_dynamic-update-slice_fusion.9
  58.0 1.1 fusion.7
  59.2 0.9 constant_dynamic-update-slice_fusion.1
  60.1 1.1 fusion.9
  61.3 0.0 reduce-scatter.3.cloned.1.call-start
  61.3 33.9 %all-reduce.7.cloned.1.call-done = (bf16[896,256]{1,0:T(8,128)(2,1)}, bf16[896,256]{1,0:T(8,128)(2,1)}) async-done(((bf16[896,256]{1,0:T(8,128)(2,1)}, bf16[896,256]{1,0:T(8,128)(2,1)}), (bf16[896,256]{1,0:T(8,128)(2,1)}, bf16[896,256]{1,0:T(8,128)(2,1)})) %all-reduce.7.cloned.1.call-update) | async-done | bytes 917520 | tf_op jit(solution)/shard_map/psum | solution.py:12
  95.2 3.1 fusion
  98.3 2.2 copy.17
  100.6 0.0 reduce-scatter.5.cloned.1.call-start
  100.6 3.1 fusion.1
  103.7 2.3 copy.18
  106.0 0.0 all-reduce.5.cloned.1.call-start
  106.1 59.1 %reduce-scatter.3.cloned.1.call-done = bf16[14,16,256]{2,1,0:T(8,128)(2,1)} async-done(((bf16[14,128,256]{2,1,0:T(8,128)(2,1)}), bf16[14,16,256]{2,1,0:T(8,128)(2,1)}) %reduce-scatter.3.cloned.1.call-update) | async-done | bytes 114704 | tf_op jit(solution)/shard_map/reduce_scatter | solution.py:45
  165.2 1.0 multiply_negate_fusion.1
  166.2 0.9 convolution_bitcast_fusion.3
  167.1 1.8 convolution_bitcast_fusion.5
  169.0 0.2 fusion.17
  169.2 0.9 convolution_add_fusion
  170.1 62.1 %reduce-scatter.5.cloned.1.call-done = bf16[14,16,256]{2,1,0:T(8,128)(2,1)} async-done(((bf16[14,128,256]{2,1,0:T(8,128)(2,1)}), bf16[14,16,256]{2,1,0:T(8,128)(2,1)}) %reduce-scatter.5.cloned.1.call-update) | async-done | bytes 114704 | tf_op jit(solution)/shard_map/reduce_scatter | solution.py:45
  232.2 1.2 multiply_negate_fusion
  233.3 0.2 convolution_bitcast_fusion.1
  233.6 0.4 copy-done.6
  234.0 0.9 fusion.5
  235.0 0.9 fusion.4
  235.9 0.9 fusion.3
  236.9 130.5 %all-reduce.5.cloned.1.call-done = (f32[256,256]{1,0:T(8,128)}, f32[256,256]{1,0:T(8,128)}, f32[256,256]{1,0:T(8,128)}) async-done(((f32[256,256]{1,0:T(8,128)}, f32[256,256]{1,0:T(8,128)}, f32[256,256]{1,0:T(8,128)}), (f32[256,256]{1,0:T(8,128)}, f32[256,256]{1,0:T(8,128)}, f32[256,256]{1,0:T(8,128)})) %all-reduce.5.cloned.1.call-update) | async-done | bytes 786448 | tf_op jit(solution)/shard_map/psum | solution.py:81
  367.3 1.1 bitcast_subtract_fusion.1
  368.4 1.3 convolution_subtract_fusion
  369.8 2.1 fusion.2
  (46 shorter events, 0.2 us)
Async XLA Ops:
  7.2 88.0 %copy-start = (bf16[1792,896]{1,0:T(8,128)(2,1)S(1)}, bf16[1792,896]{1,0:T(8,128)(2,1)}, u32[]{:S(2)}) copy-start(bf16[1792,896]{1,0:T(8,128)(2,1)} %param.8) | copy-start | bytes 9633796
  7.2 88.0 %all-reduce.7.cloned.1.call-start = ((), (), s32[]{:S(2)}) async-start(), calls=%async_computation.5 | async-start | bytes 1835008 | tf_op jit(solution)/shard_map/psum | solution.py:12
  9.3 9.4 %collective-permute-start.7 = (bf16[14,16,256]{2,1,0:T(8,128)(2,1)S(1)}, bf16[14,16,256]{2,1,0:T(8,128)(2,1)S(1)}, u32[]{:S(2)}, u32[]{:S(2)}) collective-permute-start(bf16[14,16,256]{2,1,0:T(8,128)(2,1)S(1)} %broadcast_multiply_fusion), channel_id=1, source_target_pairs={{0,1},{1,2},{2,3},{3,4},{4,5},{5,6},{6,7},{7,0},{8,9},{9,10},{10,1... | collective-permute-start | bytes 344072 | tf_op jit(solution)/shard_map/ppermute | solution.py:59
  13.3 17.2 %copy-start.7 = (bf16[14,16,256]{2,1,0:T(8,128)(2,1)}, bf16[14,16,256]{2,1,0:T(8,128)(2,1)S(1)}, u32[]{:S(2)}) copy-start(bf16[14,16,256]{2,1,0:T(8,128)(2,1)S(1)} %broadcast_multiply_fusion.1) | copy-start | bytes 344068
  13.3 10.2 %collective-permute-start = (bf16[14,16,256]{2,1,0:T(8,128)(2,1)S(1)}, bf16[14,16,256]{2,1,0:T(8,128)(2,1)S(1)}, u32[]{:S(2)}, u32[]{:S(2)}) collective-permute-start(bf16[14,16,256]{2,1,0:T(8,128)(2,1)S(1)} %broadcast_multiply_fusion.1), channel_id=1, source_target_pairs={{0,1},{1,2},{2,3},{3,4},{4,5},{5,6},{6,7},{7,0},{8,9},{9,10},{10,1... | collective-permute-start | bytes 344072 | tf_op jit(solution)/shard_map/ppermute | solution.py:59
  18.7 16.3 %copy-start.10 = (bf16[14,16,256]{2,1,0:T(8,128)(2,1)}, bf16[14,16,256]{2,1,0:T(8,128)(2,1)S(1)}, u32[]{:S(2)}) copy-start(bf16[14,16,256]{2,1,0:T(8,128)(2,1)S(1)} %collective-permute-done.7) | copy-start | bytes 344068
  18.7 9.3 %collective-permute-start.8 = (bf16[14,16,256]{2,1,0:T(8,128)(2,1)S(1)}, bf16[14,16,256]{2,1,0:T(8,128)(2,1)S(1)}, u32[]{:S(2)}, u32[]{:S(2)}) collective-permute-start(bf16[14,16,256]{2,1,0:T(8,128)(2,1)S(1)} %collective-permute-done.7), channel_id=1, source_target_pairs={{0,1},{1,2},{2,3},{3,4},{4,5},{5,6},{6,7},{7,0},{8,9},{9,10},{10,1... | collective-permute-start | bytes 344072 | tf_op jit(solution)/shard_map/ppermute | solution.py:59
  18.7 11.7 %collective-permute-start.11 = (bf16[14,16,256]{2,1,0:T(8,128)(2,1)S(1)}, bf16[14,16,256]{2,1,0:T(8,128)(2,1)}, u32[]{:S(2)}, u32[]{:S(2)}) collective-permute-start(bf16[14,16,256]{2,1,0:T(8,128)(2,1)S(1)} %broadcast_multiply_fusion), channel_id=1, source_target_pairs={{0,7},{1,0},{2,1},{3,2},{4,3},{5,4},{6,5},{7,6},{8,15},{9,8},{10,9... | collective-permute-start | bytes 344072 | tf_op jit(solution)/shard_map/ppermute | solution.py:61
  23.4 9.8 %collective-permute-start.4 = (bf16[14,16,256]{2,1,0:T(8,128)(2,1)S(1)}, bf16[14,16,256]{2,1,0:T(8,128)(2,1)S(1)}, u32[]{:S(2)}, u32[]{:S(2)}) collective-permute-start(bf16[14,16,256]{2,1,0:T(8,128)(2,1)S(1)} %broadcast_multiply_fusion.1), channel_id=1, source_target_pairs={{0,7},{1,0},{2,1},{3,2},{4,3},{5,4},{6,5},{7,6},{8,15},{9,8},{10,9... | collective-permute-start | bytes 344072 | tf_op jit(solution)/shard_map/ppermute | solution.py:61
  23.5 9.7 %copy-start.9 = (bf16[14,16,256]{2,1,0:T(8,128)(2,1)}, bf16[14,16,256]{2,1,0:T(8,128)(2,1)S(1)}, u32[]{:S(2)}) copy-start(bf16[14,16,256]{2,1,0:T(8,128)(2,1)S(1)} %collective-permute-done) | copy-start | bytes 344068
  23.5 11.5 %collective-permute-start.1 = (bf16[14,16,256]{2,1,0:T(8,128)(2,1)S(1)}, bf16[14,16,256]{2,1,0:T(8,128)(2,1)}, u32[]{:S(2)}, u32[]{:S(2)}) collective-permute-start(bf16[14,16,256]{2,1,0:T(8,128)(2,1)S(1)} %collective-permute-done), channel_id=1, source_target_pairs={{0,1},{1,2},{2,3},{3,4},{4,5},{5,6},{6,7},{7,0},{8,9},{9,10},{10,1... | collective-permute-start | bytes 344072 | tf_op jit(solution)/shard_map/ppermute | solution.py:59
  28.0 7.3 %copy-start.11 = (bf16[14,16,256]{2,1,0:T(8,128)(2,1)}, bf16[14,16,256]{2,1,0:T(8,128)(2,1)S(1)}, u32[]{:S(2)}) copy-start(bf16[14,16,256]{2,1,0:T(8,128)(2,1)S(1)} %collective-permute-done.8) | copy-start | bytes 344068
  28.0 9.7 %collective-permute-start.9 = (bf16[14,16,256]{2,1,0:T(8,128)(2,1)S(1)}, bf16[14,16,256]{2,1,0:T(8,128)(2,1)}, u32[]{:S(2)}, u32[]{:S(2)}) collective-permute-start(bf16[14,16,256]{2,1,0:T(8,128)(2,1)S(1)} %collective-permute-done.8), channel_id=1, source_target_pairs={{0,1},{1,2},{2,3},{3,4},{4,5},{5,6},{6,7},{7,0},{8,9},{9,10},{10,1... | collective-permute-start | bytes 344072 | tf_op jit(solution)/shard_map/ppermute | solution.py:59
  30.5 10.0 %collective-permute-start.12 = (bf16[14,16,256]{2,1,0:T(8,128)(2,1)}, bf16[14,16,256]{2,1,0:T(8,128)(2,1)}, u32[]{:S(2)}, u32[]{:S(2)}) collective-permute-start(bf16[14,16,256]{2,1,0:T(8,128)(2,1)} %collective-permute-done.11), channel_id=1, source_target_pairs={{0,7},{1,0},{2,1},{3,2},{4,3},{5,4},{6,5},{7,6},{8,15},{9,8},{10,9... | collective-permute-start | bytes 344072 | tf_op jit(solution)/shard_map/ppermute | solution.py:61
  33.2 11.0 %collective-permute-start.5 = (bf16[14,16,256]{2,1,0:T(8,128)(2,1)S(1)}, bf16[14,16,256]{2,1,0:T(8,128)(2,1)}, u32[]{:S(2)}, u32[]{:S(2)}) collective-permute-start(bf16[14,16,256]{2,1,0:T(8,128)(2,1)S(1)} %collective-permute-done.4), channel_id=1, source_target_pairs={{0,7},{1,0},{2,1},{3,2},{4,3},{5,4},{6,5},{7,6},{8,15},{9,8},{10,9... | collective-permute-start | bytes 344072 | tf_op jit(solution)/shard_map/ppermute | solution.py:61
  35.0 9.8 %collective-permute-start.2 = (bf16[14,16,256]{2,1,0:T(8,128)(2,1)}, bf16[14,16,256]{2,1,0:T(8,128)(2,1)}, u32[]{:S(2)}, u32[]{:S(2)}) collective-permute-start(bf16[14,16,256]{2,1,0:T(8,128)(2,1)} %collective-permute-done.1), channel_id=1, source_target_pairs={{0,1},{1,2},{2,3},{3,4},{4,5},{5,6},{6,7},{7,0},{8,9},{9,10},{10,1... | collective-permute-start | bytes 344072 | tf_op jit(solution)/shard_map/ppermute | solution.py:59
  37.6 8.6 %collective-permute-start.10 = (bf16[14,16,256]{2,1,0:T(8,128)(2,1)}, bf16[14,16,256]{2,1,0:T(8,128)(2,1)}, u32[]{:S(2)}, u32[]{:S(2)}) collective-permute-start(bf16[14,16,256]{2,1,0:T(8,128)(2,1)} %collective-permute-done.9), channel_id=1, source_target_pairs={{0,1},{1,2},{2,3},{3,4},{4,5},{5,6},{6,7},{7,0},{8,9},{9,10},{10,1... | collective-permute-start | bytes 344072 | tf_op jit(solution)/shard_map/ppermute | solution.py:59
  40.5 17.5 %collective-permute-start.13 = (bf16[14,16,256]{2,1,0:T(8,128)(2,1)}, bf16[14,16,256]{2,1,0:T(8,128)(2,1)S(1)}, u32[]{:S(2)}, u32[]{:S(2)}) collective-permute-start(bf16[14,16,256]{2,1,0:T(8,128)(2,1)} %collective-permute-done.12), channel_id=1, source_target_pairs={{0,7},{1,0},{2,1},{3,2},{4,3},{5,4},{6,5},{7,6},{8,15},{9,8},{10,9... | collective-permute-start | bytes 344072 | tf_op jit(solution)/shard_map/ppermute | solution.py:61
  44.2 15.9 %collective-permute-start.6 = (bf16[14,16,256]{2,1,0:T(8,128)(2,1)}, bf16[14,16,256]{2,1,0:T(8,128)(2,1)S(1)}, u32[]{:S(2)}, u32[]{:S(2)}) collective-permute-start(bf16[14,16,256]{2,1,0:T(8,128)(2,1)} %collective-permute-done.5), channel_id=1, source_target_pairs={{0,7},{1,0},{2,1},{3,2},{4,3},{5,4},{6,5},{7,6},{8,15},{9,8},{10,9... | collective-permute-start | bytes 344072 | tf_op jit(solution)/shard_map/ppermute | solution.py:61
  44.8 7.7 %collective-permute-start.3 = (bf16[14,16,256]{2,1,0:T(8,128)(2,1)}, bf16[14,16,256]{2,1,0:T(8,128)(2,1)S(1)}, u32[]{:S(2)}, u32[]{:S(2)}) collective-permute-start(bf16[14,16,256]{2,1,0:T(8,128)(2,1)} %collective-permute-done.2), channel_id=1, source_target_pairs={{0,1},{1,2},{2,3},{3,4},{4,5},{5,6},{6,7},{7,0},{8,9},{9,10},{10,1... | collective-permute-start | bytes 344072 | tf_op jit(solution)/shard_map/ppermute | solution.py:59
  61.3 103.9 %reduce-scatter.3.cloned.1.call-start = ((), (), s32[]{:S(2)}) async-start(), calls=%async_computation.2 | async-start | bytes 1032192 | tf_op jit(solution)/shard_map/reduce_scatter | solution.py:45
  100.6 131.6 %reduce-scatter.5.cloned.1.call-start = ((), (), s32[]{:S(2)}) async-start(), calls=%async_computation.3 | async-start | bytes 1032192 | tf_op jit(solution)/shard_map/reduce_scatter | solution.py:45
  103.7 65.3 %copy-start.1 = (bf16[256,256]{1,0:T(8,128)(2,1)S(1)}, bf16[256,256]{1,0:T(8,128)(2,1)}, u32[]{:S(2)}) copy-start(bf16[256,256]{1,0:T(8,128)(2,1)} %param.11) | copy-start | bytes 393220
  106.0 261.3 %all-reduce.5.cloned.1.call-start = ((), (), s32[]{:S(2)}) async-start(), calls=%async_computation.4 | async-start | bytes 1572864 | tf_op jit(solution)/shard_map/psum | solution.py:81
  166.2 2.8 copy-start.4
  232.2 2.8 copy-start.5
  232.2 2.8 copy-start.13
  232.2 3.7 copy-start.8
  232.2 3.7 copy-start.12
  233.3 0.7 copy-start.6
  368.4 3.5 copy-start.2
  369.7 2.2 copy-start.3
Sparse Core Ops, SparseCore 0:
  61.4 33.7 all-reduce.6
  100.7 64.4 reduce-scatter.2
  168.9 63.1 reduce-scatter.4
  238.1 129.1 all-reduce.4
